TPU v7x, 32 devices: a whole 2x2x4 slice. The times are simulated.
32 devices in a mesh: dp: 2 (over y), tensor: 4 (over z), section: 4 (over x, core).
Axes of the slice: x: 2, y: 2, z: 4, core: 2. Of those that a mesh axis runs over, the one named last changes fastest.
Arguments:
- tokens_in: bfloat16 [5120, 5120], P(('section', 'dp', 'tensor')), parts along dimension 0, may hold values from -4 to 4
- key_cot: bfloat16 [5120, 1024], P(('section', 'dp'), 'tensor'), parts along dimension 0, may hold values from -3 to 3, as said below
- row_mask: int32 [5120], P(('section', 'dp', 'tensor')), parts along dimension 0, may hold values 0 or 1
- w_key: bfloat16 [20480, 1024], P('section', 'tensor'), parts along dimension 0, may hold values from -0.078125 to 0.078125
- momentum: bfloat16 [2, 20480, 1024], P('dp', 'section', 'tensor'), parts along dimension 1, may hold values from -4 to 4
Outputs:
- input_grad: bfloat16 [5120, 5120], P(('section', 'dp', 'tensor')), parts along dimension 0
- new_momentum: bfloat16 [2, 20480, 1024], P('dp', 'section', 'tensor'), parts along dimension 1
- rollout_weight: bfloat16 [4, 20480, 256], P('tensor', 'section'), parts along dimension 1
There are 4 independent parts, one for each index of `section`. A program takes and returns all parts, laid end to end along the dimension named above; each array names one. Nothing has to cross between parts.
Inputs may be any that keep to these rules, and one draw needn't show every extreme that they name: `key_cot`: every entry is a multiple of 0.125.
All inputs are finite; a program needn't handle non-finite values. No bound on the sum of `row_mask` on one device may be relied on, other than what follows from the above.
Results may differ from a plain program's by a relative error of at most 0.017.
Values may be sent and summed in bfloat16 or wider, within the bound.
A program may use at most 128 MiB of HBM per device.

v0:
```python
import jax
import jax.numpy as jnp
from jax import lax
from jax.sharding import PartitionSpec as P

beta_slow = 0.99
beta_vote = 0.9
step_rate = 0.02


def swapped(array, axis, stride):
    return lax.ppermute(array, axis, [(i, i ^ 1 << stride) for i in range(lax.axis_size(axis))])


def unpack_words(packed):
    bit_shifts = jnp.arange(32, dtype=jnp.int32)[:, None]
    return jnp.bitwise_and(jnp.right_shift(packed[..., None, :], bit_shifts), 1)


def per_device(tokens_in, key_cot, row_mask, w_key, momentum):
    features = w_key.shape[0]
    head_cols = w_key.shape[1]
    tensor_size = lax.axis_size("tensor")
    worker_count = lax.axis_size("dp")
    mask_half = row_mask.astype(jnp.bfloat16)
    token_block = lax.all_gather(tokens_in, "tensor", axis=0, tiled=True)
    mask_block = lax.all_gather(mask_half, "tensor", axis=0, tiled=True)
    cot_block = key_cot * mask_block[:, None]
    key_grad = lax.dot_general(
        token_block, cot_block, (((0,), (0,)), ((), ())), preferred_element_type=jnp.float32
    )
    prior_momentum = momentum[0].astype(jnp.float32)
    new_momentum = (beta_slow * prior_momentum + (1.0 - beta_slow) * key_grad).astype(jnp.bfloat16)[
        None
    ]
    interp = beta_vote * prior_momentum + (1.0 - beta_vote) * key_grad
    positive = (interp > 0).astype(jnp.int32).reshape(features // 32, 32, head_cols)
    bit_shifts = jnp.arange(32, dtype=jnp.int32)[:, None]
    packed_signs = jnp.sum(jnp.left_shift(positive, bit_shifts), axis=1, dtype=jnp.int32)
    vote_count = jnp.sum(
        unpack_words(lax.all_gather(packed_signs[None], "dp", axis=0, tiled=True)),
        axis=0,
        dtype=jnp.int32,
    ).reshape(features, head_cols)
    direction = jnp.sign((2 * vote_count - worker_count).astype(jnp.float32))
    updated = (w_key.astype(jnp.float32) - step_rate * direction).astype(jnp.bfloat16)
    group_size = tensor_size // 4
    column_block = updated
    position = lax.axis_index("tensor")
    for depth_bit in range(group_size.bit_length() - 1):
        partner = swapped(column_block, "tensor", depth_bit)
        lower_half = jnp.bitwise_and(jnp.right_shift(position, depth_bit), 1) == 0
        column_block = jnp.where(
            lower_half,
            jnp.concatenate([column_block, partner], 1),
            jnp.concatenate([partner, column_block], 1),
        )
    rollout_weight = column_block[None]
    product = lax.dot_general(
        key_cot, w_key, (((1,), (1,)), ((), ())), preferred_element_type=jnp.float32
    )
    summed_grad = lax.psum_scatter(
        lax.optimization_barrier(product.astype(jnp.bfloat16))
        .astype(jnp.float32)
        .astype(jnp.bfloat16),
        "tensor",
        scatter_dimension=0,
        tiled=True,
    ).astype(jnp.float32)
    input_grad = (summed_grad * row_mask.astype(jnp.float32)[:, None]).astype(jnp.bfloat16)
    return (input_grad, new_momentum, rollout_weight)


def solution(mesh):
    return jax.shard_map(
        per_device,
        mesh=mesh,
        in_specs=(
            P(("section", "dp", "tensor"), None),
            P(("section", "dp"), "tensor"),
            P(("section", "dp", "tensor")),
            P("section", "tensor"),
            P("dp", "section", "tensor"),
        ),
        out_specs=(
            P(("section", "dp", "tensor"), None),
            P("dp", "section", "tensor"),
            P("tensor", "section", None),
        ),
        check_vma=False,
    )
```

profile of v0, /device:TPU:0, one launch (start us, length us, event | category | flops | bytes accessed | tf_op | source)
XLA Modules:
  0.0 257.5 jit_solution(211636323807559431)
XLA Ops:
  7.2 0.0 all-gather.3.cloned.1.call-start
  7.2 0.7 all-gather.3.cloned.1.call-update
  7.9 0.0 reduce-scatter.2.cloned.1.call-start
  7.9 6.5 %convolution_convert_fusion = bf16[640,5120]{1,0:T(8,128)(2,1)} fusion(bf16[640,256]{1,0:T(8,128)(2,1)} %param.6, bf16[5120,256]{1,0:T(8,128)(2,1)} %param.8), kind=kOutput, calls=%fused_computation.1 | convolution fusion | flops 1680998400 | bytes 9502720 | tf_op jit(solution)/shard_map/dot_general | solution.py:59
  14.5 0.0 reduce-scatter.2.cloned.1.call-update
  14.5 3.0 %copy.13 = bf16[1,5120,256]{1,2,0:T(8,128)(2,1)S(1)} copy(bf16[1,5120,256]{2,1,0:T(8,128)(2,1)} %param.9) | data formatting | bytes 5242880 | tf_op args[4]
  17.5 0.0 copy-done.3
  17.6 0.6 dynamic-slice
  18.8 0.0 copy-done.2
  18.8 0.2 dynamic-update-slice
  19.1 13.8 %all-reduce = bf16[640]{0:T(1024)(128)(2,1)S(1)} all-reduce(bf16[640]{0:T(1024)(128)(2,1)S(1)} %dynamic-update-slice), channel_id=1, replica_groups=mesh['dp'=2,'tensor'=4,'section'=4] {'tensor'}, use_global_device_ids=true, to_apply=%add | all-reduce | flops 640 | bytes 2560
  32.9 99.3 %all-gather.3.cloned.1.call-done = bf16[640,5120]{1,0:T(8,128)(2,1)} async-done(((bf16[160,5120]{1,0:T(8,128)(2,1)}), bf16[640,5120]{1,0:T(8,128)(2,1)}) %all-gather.3.cloned.1.call-update) | async-done | bytes 6553616 | tf_op jit(solution)/shard_map/all_gather | solution.py:26
  132.2 10.2 %fusion.7 = (s32[5120,256]{0,1:T(8,128)}, f32[256,5120]{1,0:T(8,128)}) fusion(bf16[1,5120,256]{1,2,0:T(8,128)(2,1)S(1)} %copy.13, bf16[640,5120]{1,0:T(8,128)(2,1)} %all-gather.3.cloned.1.call-done, bf16[640,256]{1,0:T(8,128)(2,1)S(1)} %copy-done.1, bf16[640]{0:T(1024)(128)(2,1)S(1)} %all-reduce), kind=kOutput, calls=%fused_computation.14 | convolution fusion | flops 1685749760 | bytes 19989760 | tf_op jit(solution)/shard_map/dot_general | solution.py:29
  142.4 5.9 %copy.14 = s32[5120,256]{1,0:T(8,128)} copy(s32[5120,256]{0,1:T(8,128)} %get-tuple-element.14) | data formatting | bytes 10485760 | tf_op jit(solution)/shard_map/reshape | solution.py:37
  148.3 4.8 %fusion.8 = bf16[1,5120,256]{1,2,0:T(8,128)(2,1)} fusion(f32[256,5120]{1,0:T(8,128)} %get-tuple-element.15, bf16[1,5120,256]{1,2,0:T(8,128)(2,1)S(1)} %copy.13), kind=kLoop, calls=%fused_computation.16 | loop fusion | flops 6553600 | bytes 10485760 | tf_op jit(solution)/shard_map/broadcast_in_dim | solution.py:33
  153.1 4.4 %copy.15 = bf16[1,5120,256]{2,1,0:T(8,128)(2,1)} copy(bf16[1,5120,256]{1,2,0:T(8,128)(2,1)} %fusion.8) | data formatting | bytes 5242880
  157.5 3.7 %shift-left_reduce_fusion = s32[160,256]{1,0:T(8,128)S(1)} fusion(s32[160,32,256]{2,1,0:T(8,128)} %bitcast.37), kind=kLoop, calls=%fused_computation.13 | loop fusion | flops 2580480 | bytes 5406720 | tf_op jit(solution)/shard_map/reduce_sum | solution.py:39
  161.2 7.3 %all-gather = s32[320,256]{1,0:T(8,128)S(1)} all-gather(s32[160,256]{1,0:T(8,128)S(1)} %shift-left_reduce_fusion), channel_id=2, replica_groups=mesh['dp'=2,'tensor'=4,'section'=4] {'dp'}, dimensions={0}, use_global_device_ids=true | all-gather | bytes 491520 | tf_op jit(solution)/shard_map/all_gather | solution.py:41
  168.5 1.7 and_reduce_fusion
  170.2 0.0 copy-start
  170.2 1.9 sign_multiply_fusion
  172.1 2.7 %fusion.6 = bf16[5120,256]{1,0:T(8,128)(2,1)} fusion(f32[160,32,256]{2,1,0:T(8,128)S(1)} %sign_multiply_fusion, bf16[5120,256]{1,0:T(8,128)(2,1)S(1)} %copy-done), kind=kLoop, calls=%fused_computation.11 | loop fusion | flops 3932160 | bytes 10485760 | tf_op jit(solution)/shard_map/convert_element_type | solution.py:46
  174.8 72.9 %reduce-scatter.2.cloned.1.call-done = bf16[160,5120]{1,0:T(8,128)(2,1)} async-done(((bf16[640,5120]{1,0:T(8,128)(2,1)}), bf16[160,5120]{1,0:T(8,128)(2,1)}) %reduce-scatter.2.cloned.1.call-update) | async-done | bytes 1638416 | tf_op jit(solution)/shard_map/reduce_scatter | solution.py:62
  247.7 3.0 %multiply_convert_fusion = bf16[160,5120]{1,0:T(8,128)(2,1)} fusion(bf16[160,5120]{1,0:T(8,128)(2,1)} %reduce-scatter.2.cloned.1.call-done, f32[160]{0:T(256)S(1)} %get-tuple-element.13), kind=kLoop, calls=%fused_computation.15 | loop fusion | flops 2457600 | bytes 3277440 | tf_op jit(solution)/shard_map/convert_element_type | solution.py:70
  (7 shorter events, 0.0 us)
Async XLA Ops:
  7.2 125.0 %all-gather.3.cloned.1.call-start = ((), (), s32[]{:S(2)}) async-start(), calls=%async_computation.2 | async-start | bytes 8192000 | tf_op jit(solution)/shard_map/all_gather | solution.py:26
  7.9 239.8 %reduce-scatter.2.cloned.1.call-start = ((), (), s32[]{:S(2)}) async-start(), calls=%async_computation.1 | async-start | bytes 8192000 | tf_op jit(solution)/shard_map/reduce_scatter | solution.py:62
  14.5 3.1 %copy-start.3 = (u32[32]{0:T(128)S(1)}, u32[32]{0:T(128)}, u32[]{:S(2)}) copy-start(u32[32]{0:T(128)} %constant.23) | copy-start | bytes 388
  14.5 4.3 %copy-start.2 = (s32[160]{0:T(256)S(1)}, s32[160]{0:T(256)}, u32[]{:S(2)}) copy-start(s32[160]{0:T(256)} %param.7) | copy-start | bytes 1924
  14.5 117.8 %copy-start.1 = (bf16[640,256]{1,0:T(8,128)(2,1)S(1)}, bf16[640,256]{1,0:T(8,128)(2,1)}, u32[]{:S(2)}) copy-start(bf16[640,256]{1,0:T(8,128)(2,1)} %param.6) | copy-start | bytes 983044
  170.2 1.9 copy-start
Sparse Core Ops, SparseCore 0:
  9.6 122.5 all-gather.2
  134.5 113.1 reduce-scatter.1
where the time goes:
time: 258 us
  waiting for transfers between devices  173 us (67%)
  blocking collectives  21.1 us (8%)
  other arithmetic  17.8 us (7%)
  matrix products  16.7 us (6%)
  between operations  14.8 us (6%)
  local copies, waits for them, and re-layouts  14.1 us (5%)
    all_gather x1, waiting for transfers between devices, per_device(): token_block = lax.all_gather(tokens_in, 'tensor', axis=0, tiled=True)  99.3 us
    reduce_scatter x1, waiting for transfers between devices, per_device(): lax.psum_scatter(lax.optimization_barrier(product.astype(jnp.bfloat16)).a...  72.9 us
    unnamed x1, blocking collectives  13.8 us
    dot_general x1, matrix products, per_device(): lax.dot_general(token_block, cot_block, (((0,), (0,)), ((), ())), preferr...  10.2 us
    unnamed x13, local copies, waits for them, and re-layouts  8.25 us
    all_gather x1, blocking collectives, per_device(): lax.all_gather(packed_signs[None], 'dp', axis=0, tiled=True)  7.26 us
    dot_general x1, matrix products, per_device(): lax.dot_general(key_cot, w_key, (((1,), (1,)), ((), ())), preferred_eleme...  6.51 us
    reshape x1, local copies, waits for them, and re-layouts, per_device(): (interp > 0).astype(jnp.int32).reshape(features // 32, 32, head_cols)  5.89 us
  transfers between devices with their start and end apart: 2, of which 2 were waited for; matrix products, arithmetic and copies ran while one was open for 18% of the time, Pallas kernels for 0%

commit v1 on v0

v1 whole, which is shorter than its diff:
```python
import functools

import jax
import jax.numpy as jnp
from jax import lax
from jax.experimental import pallas as pl
from jax.experimental.pallas import tpu as pltpu
from jax.sharding import PartitionSpec as P

beta_slow = 0.99
beta_vote = 0.9
step_rate = 0.02
MESH = pl.DeviceIdType.MESH


def swapped(array, axis, stride):
    return lax.ppermute(array, axis, [(i, i ^ 1 << stride) for i in range(lax.axis_size(axis))])


def line_kernel(
    n, workers, chunks, sub,
    tok_ref, cot_ref, mask_ref, w_ref, mom_ref,
    grad_out, mom_out, upd_out,
    gathered, sums, last_sum, total, grad_buf, mom_buf, upd_buf, votes,
    send_sem, recv_sem, vote_send, vote_recv, out_sem,
):
    z = lax.axis_index("tensor")
    worker = lax.axis_index("dp")
    rows = tok_ref.shape[0]
    width = tok_ref.shape[1] // chunks
    words = sub // 32

    barrier = pltpu.get_barrier_semaphore()

    @pl.when(z > 0)
    def _():
        pl.semaphore_signal(barrier, inc=1, device_id={"tensor": z - 1}, device_id_type=MESH)

    @pl.when(z < n - 1)
    def _():
        pl.semaphore_signal(barrier, inc=1, device_id={"tensor": z + 1}, device_id_type=MESH)

    for step in range(1, workers):
        pl.semaphore_signal(
            barrier, inc=1, device_id={"dp": lax.rem(worker + step, workers)}, device_id_type=MESH
        )

    @pl.when(jnp.logical_and(z > 0, z < n - 1))
    def _():
        pl.semaphore_wait(barrier, workers + 1)

    @pl.when(jnp.logical_or(z == 0, z == n - 1))
    def _():
        pl.semaphore_wait(barrier, workers)

    places = (z, n - 1 - z)

    def named(way, index):
        return index if way == 0 else n - 1 - index

    def block(index):
        return pl.ds(pl.multiple_of(index * rows, rows), rows)

    def columns(j):
        return pl.ds(pl.multiple_of(j * width, width), width)

    def hop(way, j, k, src, dst):
        return pltpu.make_async_remote_copy(
            src_ref=src,
            dst_ref=dst,
            send_sem=send_sem.at[way, j, k],
            recv_sem=recv_sem.at[way, j, k],
            device_id={"tensor": z + 1 if way == 0 else z - 1},
            device_id_type=MESH,
        )

    def any_hop(way, j, k):
        return hop(way, j, k, last_sum.at[j], last_sum.at[j])

    def term(j, d):
        return lax.dot_general(
            cot_ref[block(d), :], w_ref[columns(j), :],
            (((1,), (1,)), ((), ())), preferred_element_type=jnp.float32,
        )

    def send_tokens(way, j, k, shard):
        piece = gathered.at[j, block(shard)]
        hop(way, j, k, piece, piece).start()

    def send_own(j):
        gathered[j, block(z)] = (
            tok_ref[:, columns(j)].astype(jnp.float32) * mask_ref[...]
        ).astype(jnp.bfloat16)
        for way in range(2):
            @pl.when(places[way] < n - 1)
            def _():
                send_tokens(way, j, 0, z)

    def slot(j, k):
        for way in range(2):
            place = places[way]

            @pl.when(place > 0)
            def _():
                any_hop(way, j, k).wait_recv()

            @pl.when(jnp.logical_and(k + 1 <= place, place < n - 1))
            def _():
                send_tokens(way, j, k + 1, named(way, place - 1 - k))

            @pl.when(k + 1 > place)
            def _():
                d = named(way, n + place - k - 1)
                total[...] = term(j, d)

                @pl.when(place > 0)
                def _():
                    total[...] += sums[j, d].astype(jnp.float32)

                sums[j, d] = total[...].astype(jnp.bfloat16)
                src = sums.at[j, d]
                dst = last_sum.at[j] if way == 1 and k + 1 == n - 1 else src
                hop(way, j, k + 1, src, dst).start()

    def vote_copy(j, step, source):
        piece = votes.at[source, j]
        return pltpu.make_async_remote_copy(
            src_ref=piece,
            dst_ref=piece,
            send_sem=vote_send.at[step, j],
            recv_sem=vote_recv.at[step, j],
            device_id={"dp": lax.rem(worker + step, workers)},
            device_id_type=MESH,
        )

    def momentum_step(j):
        def part(i, carry):
            at = pl.ds(pl.multiple_of(j * width + i * sub, sub), sub)
            key_grad = lax.dot_general(
                gathered[j, :, pl.ds(pl.multiple_of(i * sub, sub), sub)], cot_ref[...],
                (((0,), (0,)), ((), ())), preferred_element_type=jnp.float32,
            )
            prior = mom_ref[at, :].astype(jnp.float32)
            mom_buf[at, :] = (beta_slow * prior + (1.0 - beta_slow) * key_grad).astype(jnp.bfloat16)
            interp = beta_vote * prior + (1.0 - beta_vote) * key_grad
            positive = (interp > 0).astype(jnp.int32)
            packed = positive[:words]
            for bit in range(1, 32):
                packed = packed | (positive[bit * words : (bit + 1) * words] << bit)
            votes[worker, j, pl.ds(pl.multiple_of(i * words, words), words)] = packed
            return carry

        lax.fori_loop(0, width // sub, part, 0)
        for step in range(1, workers):
            vote_copy(j, step, worker).start()
        pltpu.make_async_copy(
            mom_buf.at[columns(j)], mom_out.at[columns(j)], out_sem.at[0, j]
        ).start()

    def weight_step(j):
        for step in range(1, workers):
            vote_copy(j, step, worker).wait_recv()

        def part(i, carry):
            held = [
                votes[r, j, pl.ds(pl.multiple_of(i * words, words), words)] for r in range(workers)
            ]
            directions = []
            for bit in range(32):
                count = sum(((h >> bit) & 1) for h in held)
                twice = 2 * count - workers
                directions.append(jnp.minimum(jnp.maximum(twice, -1), 1))
            direction = jnp.concatenate(directions, 0).astype(jnp.float32)
            at = pl.ds(pl.multiple_of(j * width + i * sub, sub), sub)
            upd_buf[at, :] = (w_ref[at, :].astype(jnp.float32) - step_rate * direction).astype(
                jnp.bfloat16
            )
            return carry

        lax.fori_loop(0, width // sub, part, 0)
        pltpu.make_async_copy(
            upd_buf.at[columns(j)], upd_out.at[columns(j)], out_sem.at[1, j]
        ).start()

    def finish_grad(j):
        total[...] = term(j, z)
        for way in range(2):
            @pl.when(places[way] > 0)
            def _():
                any_hop(way, j, n - 1).wait_recv()
                came = sums[j, z] if way == 0 else last_sum[j]
                total[...] += came.astype(jnp.float32)

        grad_buf[j] = (total[...] * mask_ref[...]).astype(jnp.bfloat16)
        pltpu.make_async_copy(
            grad_buf.at[j], grad_out.at[:, columns(j)], out_sem.at[2, j]
        ).start()

    send_own(0)

    def one_chunk(j, carry):
        for k in range(n - 1):
            slot(j, k)
            if k == 0:
                @pl.when(j + 1 < chunks)
                def _():
                    send_own(j + 1)

        momentum_step(j)

        @pl.when(j > 0)
        def _():
            weight_step(j - 1)

        finish_grad(j)
        return carry

    lax.fori_loop(0, chunks, one_chunk, 0)
    weight_step(chunks - 1)

    def drain(j, carry):
        for way in range(2):
            @pl.when(places[way] < n - 1)
            def _():
                for k in range(n):
                    any_hop(way, j, k).wait_send()
        for step in range(1, workers):
            vote_copy(j, step, worker).wait_send()
        pltpu.make_async_copy(
            mom_buf.at[columns(j)], mom_out.at[columns(j)], out_sem.at[0, j]
        ).wait()
        pltpu.make_async_copy(
            upd_buf.at[columns(j)], upd_out.at[columns(j)], out_sem.at[1, j]
        ).wait()
        pltpu.make_async_copy(
            grad_buf.at[j], grad_out.at[:, columns(j)], out_sem.at[2, j]
        ).wait()
        return carry

    lax.fori_loop(0, chunks, drain, 0)


def per_device(tokens_in, key_cot, row_mask, w_key, momentum):
    rows, features = tokens_in.shape
    head_cols = w_key.shape[1]
    n = lax.axis_size("tensor")
    workers = lax.axis_size("dp")
    sub = 256
    chunks = 5
    width = features // chunks
    bf16 = jnp.bfloat16
    vmem = pl.BlockSpec(memory_space=pltpu.VMEM)
    hbm = pl.BlockSpec(memory_space=pl.ANY)
    dma = pltpu.SemaphoreType.DMA
    input_grad, new_momentum, updated = pl.pallas_call(
        functools.partial(line_kernel, n, workers, chunks, sub),
        out_shape=(
            jax.ShapeDtypeStruct((rows, features), bf16),
            jax.ShapeDtypeStruct((features, head_cols), bf16),
            jax.ShapeDtypeStruct((features, head_cols), bf16),
        ),
        in_specs=[vmem] * 5,
        out_specs=(hbm, hbm, hbm),
        scratch_shapes=[
            pltpu.VMEM((chunks, n * rows, width), bf16),
            pltpu.VMEM((chunks, n, rows, width), bf16),
            pltpu.VMEM((chunks, rows, width), bf16),
            pltpu.VMEM((rows, width), jnp.float32),
            pltpu.VMEM((chunks, rows, width), bf16),
            pltpu.VMEM((features, head_cols), bf16),
            pltpu.VMEM((features, head_cols), bf16),
            pltpu.VMEM((workers, chunks, width // 32, head_cols), jnp.int32),
            dma((2, chunks, n)),
            dma((2, chunks, n)),
            dma((workers, chunks)),
            dma((workers, chunks)),
            dma((3, chunks)),
        ],
        compiler_params=pltpu.CompilerParams(
            collective_id=0, has_side_effects=True, vmem_limit_bytes=56 * 2**20
        ),
        cost_estimate=pl.CostEstimate(
            flops=4 * n * rows * features * head_cols,
            bytes_accessed=2 * (2 * rows * features + 4 * features * head_cols),
            transcendentals=0,
        ),
    )(tokens_in, key_cot, row_mask.astype(jnp.float32)[:, None], w_key, momentum[0])
    column_block = updated
    position = lax.axis_index("tensor")
    for depth_bit in range((n // 4).bit_length() - 1):
        partner = swapped(column_block, "tensor", depth_bit)
        lower_half = jnp.bitwise_and(jnp.right_shift(position, depth_bit), 1) == 0
        column_block = jnp.where(
            lower_half,
            jnp.concatenate([column_block, partner], 1),
            jnp.concatenate([partner, column_block], 1),
        )
    return (input_grad, new_momentum[None], column_block[None])


def solution(mesh):
    return jax.shard_map(
        per_device,
        mesh=mesh,
        in_specs=(
            P(("section", "dp", "tensor"), None),
            P(("section", "dp"), "tensor"),
            P(("section", "dp", "tensor")),
            P("section", "tensor"),
            P("dp", "section", "tensor"),
        ),
        out_specs=(
            P(("section", "dp", "tensor"), None),
            P("dp", "section", "tensor"),
            P("tensor", "section", None),
        ),
        check_vma=False,
    )
```

time: 258 us -> 172 us (0.67)
  waiting for transfers between devices: 173 us -> 0 us
  Pallas kernels: 0 us -> 163 us
  blocking collectives: 21.1 us -> 0 us
  other arithmetic: 17.8 us -> 0.68 us
  matrix products: 16.7 us -> 0 us
  between operations: 14.8 us -> 0.65 us
  local copies, waits for them, and re-layouts: 14.1 us -> 7.79 us
    pallas_call x0 -> x1, Pallas kernels: none -> 163 us  [per_device(): pl.pallas_call(functools.partial(line_kernel, n, workers, chunks, sub), o...]
    all_gather x1 -> x0, waiting for transfers between devices: 99.3 us -> none  [per_device(): token_block = lax.all_gather(tokens_in, 'tensor', axis=0, tiled=True)]
    reduce_scatter x1 -> x0, waiting for transfers between devices: 72.9 us -> none  [per_device(): lax.psum_scatter(lax.optimization_barrier(product.astype(jnp.bfloat16)).a...]
    dot_general x2 -> x0, matrix products: 16.7 us -> none  [the longest x1 10.2 us: per_device(): lax.dot_general(token_block, cot_block, (((0,), (0,)), ((), ())), preferr...]
    unnamed x1 -> x0, blocking collectives: 13.8 us -> none
    all_gather x1 -> x0, blocking collectives: 7.26 us -> none  [per_device(): lax.all_gather(packed_signs[None], 'dp', axis=0, tiled=True)]
    reshape x1 -> x0, local copies, waits for them, and re-layouts: 5.89 us -> none  [per_device(): (interp > 0).astype(jnp.int32).reshape(features // 32, 32, head_cols)]
    reduce_sum x2 -> x0, other arithmetic: 5.44 us -> none  [the longest x1 3.71 us: per_device(): jnp.sum(jnp.left_shift(positive, bit_shifts), axis=1, dtype=jnp.int32)]
  transfers between devices with their start and end apart: 2 -> 0, of which waited for: 2 -> 0; matrix products, arithmetic and copies ran while one was open for 18% -> 0% of each run, Pallas kernels for 0% -> 0%
where the time goes in v1:
time: 172 us
  Pallas kernels  163 us (95%)
  local copies, waits for them, and re-layouts  7.79 us (5%)
    pallas_call x1, Pallas kernels, per_device(): pl.pallas_call(functools.partial(line_kernel, n, workers, chunks, sub), o...  163 us
    unnamed x7, local copies, waits for them, and re-layouts  7.03 us

profile of v1, /device:TPU:0, one launch (start us, length us, event | category | flops | bytes accessed | tf_op | source)
XLA Modules:
  0.0 171.9 jit_solution(1654110061585113672)
XLA Ops:
  0.6 0.7 convert_element_type.3
  1.3 0.8 copy.8.mask_ref
  2.1 162.8 %shard_map.76 = (bf16[160,5120]{1,0:T(8,128)(2,1)}, bf16[5120,256]{1,0:T(8,128)(2,1)}, bf16[5120,256]{1,0:T(8,128)(2,1)}) custom-call(bf16[160,5120]{1,0:T(8,128)(2,1)} %tok_ref.1, bf16[640,256]{1,0:T(8,128)(2,1)} %cot_ref.1, f32[160,1]{1,0:T(8,128)} %copy.8.mask_ref, bf16[5120,256]{1,0:T(8,128)(2,1)} %w_ref.1, bf16[5120,256]{1,0:T(8,128)(2,1)} %bitcast.7), custom_call_target="tpu_custom_call" | custom-call | flops 3355443200 | bytes 13762560 | tf_op jit(solution)/shard_map/pallas_call | solution.py:255
  164.8 0.0 copy-start.1
  164.8 2.9 %copy.12 = bf16[160,5120]{1,0:T(8,128)(2,1)} copy(bf16[160,5120]{1,0:T(8,128)(2,1)} %get-tuple-element.12) | data formatting | bytes 3276800
  167.7 0.0 copy-done.1
  167.7 0.0 copy-start
  167.7 1.5 copy.13
  169.2 1.2 copy-done
  170.4 1.5 copy.14
Async XLA Ops:
  164.8 2.9 %copy-start.1 = (bf16[5120,256]{1,0:T(8,128)(2,1)S(1)}, bf16[5120,256]{1,0:T(8,128)(2,1)}, u32[]{:S(2)}) copy-start(bf16[5120,256]{1,0:T(8,128)(2,1)} %get-tuple-element.7) | copy-start | bytes 7864324
  167.7 2.7 %copy-start = (bf16[5120,256]{1,0:T(8,128)(2,1)S(1)}, bf16[5120,256]{1,0:T(8,128)(2,1)}, u32[]{:S(2)}) copy-start(bf16[5120,256]{1,0:T(8,128)(2,1)} %get-tuple-element.8) | copy-start | bytes 7864324

commit v2 on v1

--- a/solution.py
+++ b/solution.py
@@ -18,14 +18,23 @@
 
 
 def line_kernel(
-    n, workers, chunks, sub,
-    tok_ref, cot_ref, mask_ref, w_ref, mom_ref,
+    n, workers, chunks, lanes, sub,
+    tok_in, cot_in, mask_ref, w_in, mom_in,
     grad_out, mom_out, upd_out,
+    tok_ref, cot_ref, w_ref, mom_ref,
     gathered, sums, last_sum, total, grad_buf, mom_buf, upd_buf, votes,
-    send_sem, recv_sem, vote_send, vote_recv, out_sem,
+    send_sem, recv_sem, vote_send, vote_recv, out_sem, in_sem,
 ):
     z = lax.axis_index("tensor")
     worker = lax.axis_index("dp")
+    loads = [
+        pltpu.make_async_copy(src, dst, in_sem.at[i])
+        for i, (src, dst) in enumerate(
+            ((tok_in, tok_ref), (cot_in, cot_ref), (w_in, w_ref), (mom_in, mom_ref))
+        )
+    ]
+    for load in loads:
+        load.start()
     rows = tok_ref.shape[0]
     width = tok_ref.shape[1] // chunks
     words = sub // 32
@@ -196,27 +205,47 @@
             grad_buf.at[j], grad_out.at[:, columns(j)], out_sem.at[2, j]
         ).start()
 
-    send_own(0)
-
-    def one_chunk(j, carry):
+    def each(function, group):
+        def one(half, carry):
+            function(group * lanes + half)
+            return carry
+
+        lax.fori_loop(0, lanes, one, 0)
+
+    groups = chunks // lanes
+    loads[0].wait()
+    each(send_own, 0)
+    for load in loads[1:]:
+        load.wait()
+
+    def one_group(group, carry):
         for k in range(n - 1):
-            slot(j, k)
+            each(lambda j: slot(j, k), group)
             if k == 0:
-                @pl.when(j + 1 < chunks)
-                def _():
-                    send_own(j + 1)
-
-        momentum_step(j)
-
-        @pl.when(j > 0)
-        def _():
-            weight_step(j - 1)
-
-        finish_grad(j)
+                @pl.when(group + 1 < groups)
+                def _():
+                    each(send_own, group + 1)
+
+                @pl.when(group > 0)
+                def _():
+                    each(momentum_step, group - 1)
+
+                @pl.when(group > 1)
+                def _():
+                    each(weight_step, group - 2)
+
+                @pl.when(group > 0)
+                def _():
+                    each(finish_grad, group - 1)
+
         return carry
 
-    lax.fori_loop(0, chunks, one_chunk, 0)
-    weight_step(chunks - 1)
+    lax.fori_loop(0, groups, one_group, 0)
+    each(momentum_step, groups - 1)
+    if groups > 1:
+        each(weight_step, groups - 2)
+    each(weight_step, groups - 1)
+    each(finish_grad, groups - 1)
 
     def drain(j, carry):
         for way in range(2):
@@ -246,22 +275,27 @@
     n = lax.axis_size("tensor")
     workers = lax.axis_size("dp")
     sub = 256
-    chunks = 5
+    chunks = 10
+    lanes = 2
     width = features // chunks
     bf16 = jnp.bfloat16
     vmem = pl.BlockSpec(memory_space=pltpu.VMEM)
     hbm = pl.BlockSpec(memory_space=pl.ANY)
     dma = pltpu.SemaphoreType.DMA
     input_grad, new_momentum, updated = pl.pallas_call(
-        functools.partial(line_kernel, n, workers, chunks, sub),
+        functools.partial(line_kernel, n, workers, chunks, lanes, sub),
         out_shape=(
             jax.ShapeDtypeStruct((rows, features), bf16),
             jax.ShapeDtypeStruct((features, head_cols), bf16),
             jax.ShapeDtypeStruct((features, head_cols), bf16),
         ),
-        in_specs=[vmem] * 5,
+        in_specs=[hbm, hbm, vmem, hbm, hbm],
         out_specs=(hbm, hbm, hbm),
         scratch_shapes=[
+            pltpu.VMEM((rows, features), bf16),
+            pltpu.VMEM(key_cot.shape, bf16),
+            pltpu.VMEM((features, head_cols), bf16),
+            pltpu.VMEM((features, head_cols), bf16),
             pltpu.VMEM((chunks, n * rows, width), bf16),
             pltpu.VMEM((chunks, n, rows, width), bf16),
             pltpu.VMEM((chunks, rows, width), bf16),
@@ -275,6 +309,7 @@
             dma((workers, chunks)),
             dma((workers, chunks)),
             dma((3, chunks)),
+            dma((4,)),
         ],
         compiler_params=pltpu.CompilerParams(
             collective_id=0, has_side_effects=True, vmem_limit_bytes=56 * 2**20

time: 172 us -> 159 us (0.924)
  Pallas kernels: 163 us -> 149 us
    pallas_call x1, Pallas kernels: 163 us -> 149 us  [per_device(): pl.pallas_call(functools.partial(line_kernel, n, workers, chunks, lanes,...]
where the time goes in v2:
time: 159 us
  Pallas kernels  149 us (94%)
  local copies, waits for them, and re-layouts  7.79 us (5%)
    pallas_call x1, Pallas kernels, per_device(): pl.pallas_call(functools.partial(line_kernel, n, workers, chunks, lanes,...  149 us
    unnamed x7, local copies, waits for them, and re-layouts  7.03 us

profile of v2, /device:TPU:0, one launch (start us, length us, event | category | flops | bytes accessed | tf_op | source)
XLA Modules:
  0.0 158.6 jit_solution(10618827193999799483)
XLA Ops:
  0.6 0.7 convert_element_type.3
  1.3 0.8 copy.8.mask_ref
  2.1 149.5 %shard_map.76 = (bf16[160,5120]{1,0:T(8,128)(2,1)}, bf16[5120,256]{1,0:T(8,128)(2,1)}, bf16[5120,256]{1,0:T(8,128)(2,1)}) custom-call(bf16[160,5120]{1,0:T(8,128)(2,1)} %tok_in.1, bf16[640,256]{1,0:T(8,128)(2,1)} %cot_in.1, f32[160,1]{1,0:T(8,128)} %copy.8.mask_ref, bf16[5120,256]{1,0:T(8,128)(2,1)} %w_in.1, bf16[5120,256]{1,0:T(8,128)(2,1)} %bitcast.7), custom_call_target="tpu_custom_call" | custom-call | flops 3355443200 | bytes 13762560 | tf_op jit(solution)/shard_map/pallas_call | solution.py:285
  151.5 0.0 copy-start.1
  151.6 2.9 %copy.12 = bf16[160,5120]{1,0:T(8,128)(2,1)} copy(bf16[160,5120]{1,0:T(8,128)(2,1)} %get-tuple-element.12) | data formatting | bytes 3276800
  154.4 0.0 copy-done.1
  154.4 0.0 copy-start
  154.4 1.5 copy.13
  155.9 1.2 copy-done
  157.1 1.5 copy.14
Async XLA Ops:
  151.5 2.9 %copy-start.1 = (bf16[5120,256]{1,0:T(8,128)(2,1)S(1)}, bf16[5120,256]{1,0:T(8,128)(2,1)}, u32[]{:S(2)}) copy-start(bf16[5120,256]{1,0:T(8,128)(2,1)} %get-tuple-element.7) | copy-start | bytes 7864324
  154.4 2.7 %copy-start = (bf16[5120,256]{1,0:T(8,128)(2,1)S(1)}, bf16[5120,256]{1,0:T(8,128)(2,1)}, u32[]{:S(2)}) copy-start(bf16[5120,256]{1,0:T(8,128)(2,1)} %get-tuple-element.8) | copy-start | bytes 7864324

commit v3 on v2

--- a/solution.py
+++ b/solution.py
@@ -22,8 +22,8 @@
     tok_in, cot_in, mask_ref, w_in, mom_in,
     grad_out, mom_out, upd_out,
     tok_ref, cot_ref, w_ref, mom_ref,
-    gathered, sums, last_sum, total, grad_buf, mom_buf, upd_buf, votes,
-    send_sem, recv_sem, vote_send, vote_recv, out_sem, in_sem,
+    gathered, sums, last_sum, total, votes,
+    send_sem, recv_sem, vote_send, vote_recv, in_sem,
 ):
     z = lax.axis_index("tensor")
     worker = lax.axis_index("dp")
@@ -150,7 +150,7 @@
                 (((0,), (0,)), ((), ())), preferred_element_type=jnp.float32,
             )
             prior = mom_ref[at, :].astype(jnp.float32)
-            mom_buf[at, :] = (beta_slow * prior + (1.0 - beta_slow) * key_grad).astype(jnp.bfloat16)
+            mom_out[at, :] = (beta_slow * prior + (1.0 - beta_slow) * key_grad).astype(jnp.bfloat16)
             interp = beta_vote * prior + (1.0 - beta_vote) * key_grad
             positive = (interp > 0).astype(jnp.int32)
             packed = positive[:words]
@@ -162,9 +162,6 @@
         lax.fori_loop(0, width // sub, part, 0)
         for step in range(1, workers):
             vote_copy(j, step, worker).start()
-        pltpu.make_async_copy(
-            mom_buf.at[columns(j)], mom_out.at[columns(j)], out_sem.at[0, j]
-        ).start()
 
     def weight_step(j):
         for step in range(1, workers):
@@ -181,15 +178,12 @@
                 directions.append(jnp.minimum(jnp.maximum(twice, -1), 1))
             direction = jnp.concatenate(directions, 0).astype(jnp.float32)
             at = pl.ds(pl.multiple_of(j * width + i * sub, sub), sub)
-            upd_buf[at, :] = (w_ref[at, :].astype(jnp.float32) - step_rate * direction).astype(
+            upd_out[at, :] = (w_ref[at, :].astype(jnp.float32) - step_rate * direction).astype(
                 jnp.bfloat16
             )
             return carry
 
         lax.fori_loop(0, width // sub, part, 0)
-        pltpu.make_async_copy(
-            upd_buf.at[columns(j)], upd_out.at[columns(j)], out_sem.at[1, j]
-        ).start()
 
     def finish_grad(j):
         total[...] = term(j, z)
@@ -200,10 +194,7 @@
                 came = sums[j, z] if way == 0 else last_sum[j]
                 total[...] += came.astype(jnp.float32)
 
-        grad_buf[j] = (total[...] * mask_ref[...]).astype(jnp.bfloat16)
-        pltpu.make_async_copy(
-            grad_buf.at[j], grad_out.at[:, columns(j)], out_sem.at[2, j]
-        ).start()
+        grad_out[:, columns(j)] = (total[...] * mask_ref[...]).astype(jnp.bfloat16)
 
     def each(function, group):
         def one(half, carry):
@@ -255,15 +246,6 @@
                     any_hop(way, j, k).wait_send()
         for step in range(1, workers):
             vote_copy(j, step, worker).wait_send()
-        pltpu.make_async_copy(
-            mom_buf.at[columns(j)], mom_out.at[columns(j)], out_sem.at[0, j]
-        ).wait()
-        pltpu.make_async_copy(
-            upd_buf.at[columns(j)], upd_out.at[columns(j)], out_sem.at[1, j]
-        ).wait()
-        pltpu.make_async_copy(
-            grad_buf.at[j], grad_out.at[:, columns(j)], out_sem.at[2, j]
-        ).wait()
         return carry
 
     lax.fori_loop(0, chunks, drain, 0)
@@ -285,12 +267,12 @@
     input_grad, new_momentum, updated = pl.pallas_call(
         functools.partial(line_kernel, n, workers, chunks, lanes, sub),
         out_shape=(
-            jax.ShapeDtypeStruct((rows, features), bf16),
-            jax.ShapeDtypeStruct((features, head_cols), bf16),
-            jax.ShapeDtypeStruct((features, head_cols), bf16),
+            pltpu.VMEM((rows, features), bf16),
+            pltpu.VMEM((features, head_cols), bf16),
+            pltpu.VMEM((features, head_cols), bf16),
         ),
         in_specs=[hbm, hbm, vmem, hbm, hbm],
-        out_specs=(hbm, hbm, hbm),
+        out_specs=(vmem, vmem, vmem),
         scratch_shapes=[
             pltpu.VMEM((rows, features), bf16),
             pltpu.VMEM(key_cot.shape, bf16),
@@ -300,15 +282,11 @@
             pltpu.VMEM((chunks, n, rows, width), bf16),
             pltpu.VMEM((chunks, rows, width), bf16),
             pltpu.VMEM((rows, width), jnp.float32),
-            pltpu.VMEM((chunks, rows, width), bf16),
-            pltpu.VMEM((features, head_cols), bf16),
-            pltpu.VMEM((features, head_cols), bf16),
             pltpu.VMEM((workers, chunks, width // 32, head_cols), jnp.int32),
             dma((2, chunks, n)),
             dma((2, chunks, n)),
             dma((workers, chunks)),
             dma((workers, chunks)),
-            dma((3, chunks)),
             dma((4,)),
         ],
         compiler_params=pltpu.CompilerParams(

time: 159 us -> 155 us (0.975)
  local copies, waits for them, and re-layouts: 7.79 us -> 4.91 us
    unnamed x7 -> x3, local copies, waits for them, and re-layouts: 7.03 us -> 4.15 us
where the time goes in v3:
time: 155 us
  Pallas kernels  149 us (96%)
  local copies, waits for them, and re-layouts  4.91 us (3%)
    pallas_call x1, Pallas kernels, per_device(): pl.pallas_call(functools.partial(line_kernel, n, workers, chunks, lanes,...  149 us
    unnamed x3, local copies, waits for them, and re-layouts  4.15 us

profile of v3, /device:TPU:0, one launch (start us, length us, event | category | flops | bytes accessed | tf_op | source)
XLA Modules:
  0.0 154.9 jit_solution(13011432966938676916)
XLA Ops:
  0.6 0.7 convert_element_type.3
  1.3 0.8 copy.8.mask_ref
  2.1 148.7 %shard_map.76 = (bf16[160,5120]{1,0:T(8,128)(2,1)S(1)}, bf16[5120,256]{1,0:T(8,128)(2,1)S(1)}, bf16[5120,256]{1,0:T(8,128)(2,1)S(1)}) custom-call(bf16[160,5120]{1,0:T(8,128)(2,1)} %tok_in.1, bf16[640,256]{1,0:T(8,128)(2,1)} %cot_in.1, f32[160,1]{1,0:T(8,128)} %copy.8.mask_ref, bf16[5120,256]{1,0:T(8,128)(2,1)} %w_in.1, bf16[5120,256]{1,0:T(8,128)(2,1)} %bitcast.7), custom_call_target="tpu_custom_call" | custom-call | flops 3355443200 | bytes 13762560 | tf_op jit(solution)/shard_map/pallas_call | solution.py:267
  150.7 1.2 copy.12
  151.9 1.5 copy.13
  153.4 1.5 copy.14

commit v4 on v3

--- a/solution.py
+++ b/solution.py
@@ -19,9 +19,9 @@
 
 def line_kernel(
     n, workers, chunks, lanes, sub,
-    tok_in, cot_in, mask_ref, w_in, mom_in,
+    tok_in, cot_in, mask_in, w_in, mom_in,
     grad_out, mom_out, upd_out,
-    tok_ref, cot_ref, w_ref, mom_ref,
+    tok_ref, cot_ref, w_ref, mom_ref, mask_ref,
     gathered, sums, last_sum, total, votes,
     send_sem, recv_sem, vote_send, vote_recv, in_sem,
 ):
@@ -54,14 +54,6 @@
             barrier, inc=1, device_id={"dp": lax.rem(worker + step, workers)}, device_id_type=MESH
         )
 
-    @pl.when(jnp.logical_and(z > 0, z < n - 1))
-    def _():
-        pl.semaphore_wait(barrier, workers + 1)
-
-    @pl.when(jnp.logical_or(z == 0, z == n - 1))
-    def _():
-        pl.semaphore_wait(barrier, workers)
-
     places = (z, n - 1 - z)
 
     def named(way, index):
@@ -96,10 +88,12 @@
         piece = gathered.at[j, block(shard)]
         hop(way, j, k, piece, piece).start()
 
-    def send_own(j):
+    def mask_own(j):
         gathered[j, block(z)] = (
             tok_ref[:, columns(j)].astype(jnp.float32) * mask_ref[...]
         ).astype(jnp.bfloat16)
+
+    def send_own(j):
         for way in range(2):
             @pl.when(places[way] < n - 1)
             def _():
@@ -204,7 +198,23 @@
         lax.fori_loop(0, lanes, one, 0)
 
     groups = chunks // lanes
+    square = (rows, rows)
+    diagonal = lax.broadcasted_iota(jnp.int32, square, 0) == lax.broadcasted_iota(
+        jnp.int32, square, 1
+    )
+    spread = jnp.broadcast_to(mask_in[...].astype(jnp.float32), square)
+    mask_ref[...] = jnp.sum(jnp.where(diagonal, spread, 0.0), axis=1, keepdims=True)
     loads[0].wait()
+    each(mask_own, 0)
+
+    @pl.when(jnp.logical_and(z > 0, z < n - 1))
+    def _():
+        pl.semaphore_wait(barrier, workers + 1)
+
+    @pl.when(jnp.logical_or(z == 0, z == n - 1))
+    def _():
+        pl.semaphore_wait(barrier, workers)
+
     each(send_own, 0)
     for load in loads[1:]:
         load.wait()
@@ -215,26 +225,22 @@
             if k == 0:
                 @pl.when(group + 1 < groups)
                 def _():
+                    each(mask_own, group + 1)
                     each(send_own, group + 1)
 
-                @pl.when(group > 0)
-                def _():
+            @pl.when(group > 0)
+            def _():
+                if k == 0:
                     each(momentum_step, group - 1)
-
-                @pl.when(group > 1)
-                def _():
-                    each(weight_step, group - 2)
-
-                @pl.when(group > 0)
-                def _():
+                if k == min(1, n - 2):
                     each(finish_grad, group - 1)
+                if k == n - 2:
+                    each(weight_step, group - 1)
 
         return carry
 
     lax.fori_loop(0, groups, one_group, 0)
     each(momentum_step, groups - 1)
-    if groups > 1:
-        each(weight_step, groups - 2)
     each(weight_step, groups - 1)
     each(finish_grad, groups - 1)
 
@@ -249,6 +255,35 @@
         return carry
 
     lax.fori_loop(0, chunks, drain, 0)
+
+
+def store_kernel(pieces, *refs):
+    count = len(refs) // 2
+    sem = refs[-1]
+    copies = []
+    for source, target in zip(refs[:count], refs[count : 2 * count]):
+        step = source.shape[0] // pieces
+        for piece in range(pieces):
+            at = pl.ds(piece * step, step)
+            copies.append(
+                pltpu.make_async_copy(source.at[at], target.at[at], sem.at[len(copies)])
+            )
+    for copy in copies:
+        copy.start()
+    for copy in copies:
+        copy.wait()
+
+
+def stored(*arrays):
+    pieces = 2
+    return pl.pallas_call(
+        functools.partial(store_kernel, pieces),
+        out_shape=tuple(jax.ShapeDtypeStruct(a.shape, a.dtype) for a in arrays),
+        in_specs=[pl.BlockSpec(memory_space=pltpu.VMEM)] * len(arrays),
+        out_specs=tuple(pl.BlockSpec(memory_space=pl.ANY) for _ in arrays),
+        scratch_shapes=[pltpu.SemaphoreType.DMA((pieces * len(arrays),))],
+        compiler_params=pltpu.CompilerParams(vmem_limit_bytes=16 * 2**20),
+    )(*arrays)
 
 
 def per_device(tokens_in, key_cot, row_mask, w_key, momentum):
@@ -278,6 +313,7 @@
             pltpu.VMEM(key_cot.shape, bf16),
             pltpu.VMEM((features, head_cols), bf16),
             pltpu.VMEM((features, head_cols), bf16),
+            pltpu.VMEM((rows, 1), jnp.float32),
             pltpu.VMEM((chunks, n * rows, width), bf16),
             pltpu.VMEM((chunks, n, rows, width), bf16),
             pltpu.VMEM((chunks, rows, width), bf16),
@@ -297,7 +333,8 @@
             bytes_accessed=2 * (2 * rows * features + 4 * features * head_cols),
             transcendentals=0,
         ),
-    )(tokens_in, key_cot, row_mask.astype(jnp.float32)[:, None], w_key, momentum[0])
+    )(tokens_in, key_cot, row_mask[None], w_key, momentum[0])
+    input_grad, new_momentum, updated = stored(input_grad, new_momentum, updated)
     column_block = updated
     position = lax.axis_index("tensor")
     for depth_bit in range((n // 4).bit_length() - 1):

time: 155 us -> 152 us (0.981)
  local copies, waits for them, and re-layouts: 4.91 us -> 0 us
  Pallas kernels: 149 us -> 151 us
    unnamed x3 -> x0, local copies, waits for them, and re-layouts: 4.15 us -> none
    pallas_call x0 -> x1, Pallas kernels: none -> 2.91 us  [stored(): pl.pallas_call(functools.partial(store_kernel, pieces), out_shape=tuple((...]
where the time goes in v4:
time: 152 us
  Pallas kernels  151 us (99%)
    pallas_call x1, Pallas kernels, per_device(): pl.pallas_call(functools.partial(line_kernel, n, workers, chunks, lanes,...  149 us

profile of v4, /device:TPU:0, one launch (start us, length us, event | category | flops | bytes accessed | tf_op | source)
XLA Modules:
  0.0 152.1 jit_solution(15389308991631876049)
XLA Ops:
  0.6 148.6 %shard_map.76 = (bf16[160,5120]{1,0:T(8,128)(2,1)S(1)}, bf16[5120,256]{1,0:T(8,128)(2,1)S(1)}, bf16[5120,256]{1,0:T(8,128)(2,1)S(1)}) custom-call(bf16[160,5120]{1,0:T(8,128)(2,1)} %tok_in.1, bf16[640,256]{1,0:T(8,128)(2,1)} %cot_in.1, s32[1,160]{1,0:T(1,128)} %bitcast.7, bf16[5120,256]{1,0:T(8,128)(2,1)} %w_in.1, bf16[5120,256]{1,0:T(8,128)(2,1)} %bitcast.4), custom_call_target="tpu_custom_call" | custom-call | flops 3355443200 | bytes 13762560 | tf_op jit(solution)/shard_map/pallas_call | solution.py:302
  149.2 2.9 %shard_map.77 = (bf16[160,5120]{1,0:T(8,128)(2,1)}, bf16[5120,256]{1,0:T(8,128)(2,1)}, bf16[5120,256]{1,0:T(8,128)(2,1)}) custom-call(bf16[160,5120]{1,0:T(8,128)(2,1)S(1)} %get-tuple-element.9.refs_0_, bf16[5120,256]{1,0:T(8,128)(2,1)S(1)} %get-tuple-element.10.refs_1_, bf16[5120,256]{1,0:T(8,128)(2,1)S(1)} %get-tuple-element.11.refs_2_), custom_call_target="tpu_custom_call" | custom-call | tf_op jit(solution)/shard_map/pallas_call | solution.py:279

commit v5 on v4

--- a/solution.py
+++ b/solution.py
@@ -18,7 +18,7 @@
 
 
 def line_kernel(
-    n, workers, chunks, lanes, sub,
+    n, workers, chunks, lanes, ahead, sub,
     tok_in, cot_in, mask_in, w_in, mom_in,
     grad_out, mom_out, upd_out,
     tok_ref, cot_ref, w_ref, mom_ref, mask_ref,
@@ -205,7 +205,8 @@
     spread = jnp.broadcast_to(mask_in[...].astype(jnp.float32), square)
     mask_ref[...] = jnp.sum(jnp.where(diagonal, spread, 0.0), axis=1, keepdims=True)
     loads[0].wait()
-    each(mask_own, 0)
+    for group in range(ahead):
+        each(mask_own, group)
 
     @pl.when(jnp.logical_and(z > 0, z < n - 1))
     def _():
@@ -215,7 +216,8 @@
     def _():
         pl.semaphore_wait(barrier, workers)
 
-    each(send_own, 0)
+    for group in range(ahead):
+        each(send_own, group)
     for load in loads[1:]:
         load.wait()
 
@@ -223,10 +225,10 @@
         for k in range(n - 1):
             each(lambda j: slot(j, k), group)
             if k == 0:
-                @pl.when(group + 1 < groups)
+                @pl.when(group + ahead < groups)
                 def _():
-                    each(mask_own, group + 1)
-                    each(send_own, group + 1)
+                    each(mask_own, group + ahead)
+                    each(send_own, group + ahead)
 
             @pl.when(group > 0)
             def _():
@@ -292,7 +294,8 @@
     n = lax.axis_size("tensor")
     workers = lax.axis_size("dp")
     sub = 256
-    chunks = 10
+    chunks = 20
+    ahead = 2
     lanes = 2
     width = features // chunks
     bf16 = jnp.bfloat16
@@ -300,7 +303,7 @@
     hbm = pl.BlockSpec(memory_space=pl.ANY)
     dma = pltpu.SemaphoreType.DMA
     input_grad, new_momentum, updated = pl.pallas_call(
-        functools.partial(line_kernel, n, workers, chunks, lanes, sub),
+        functools.partial(line_kernel, n, workers, chunks, lanes, ahead, sub),
         out_shape=(
             pltpu.VMEM((rows, features), bf16),
             pltpu.VMEM((features, head_cols), bf16),

time: 152 us -> 161 us (1.059)
  Pallas kernels: 151 us -> 160 us
    pallas_call x1, Pallas kernels: 149 us -> 157 us  [per_device(): pl.pallas_call(functools.partial(line_kernel, n, workers, chunks, lanes,...]
where the time goes in v5:
time: 161 us
  Pallas kernels  160 us (99%)
    pallas_call x1, Pallas kernels, per_device(): pl.pallas_call(functools.partial(line_kernel, n, workers, chunks, lanes,...  157 us

profile of v5, /device:TPU:0, one launch (start us, length us, event | category | flops | bytes accessed | tf_op | source)
XLA Modules:
  0.0 160.7 jit_solution(9851757602216217280)
XLA Ops:
  0.6 157.2 %shard_map.76 = (bf16[160,5120]{1,0:T(8,128)(2,1)S(1)}, bf16[5120,256]{1,0:T(8,128)(2,1)S(1)}, bf16[5120,256]{1,0:T(8,128)(2,1)S(1)}) custom-call(bf16[160,5120]{1,0:T(8,128)(2,1)} %tok_in.1, bf16[640,256]{1,0:T(8,128)(2,1)} %cot_in.1, s32[1,160]{1,0:T(1,128)} %bitcast.7, bf16[5120,256]{1,0:T(8,128)(2,1)} %w_in.1, bf16[5120,256]{1,0:T(8,128)(2,1)} %bitcast.4), custom_call_target="tpu_custom_call" | custom-call | flops 3355443200 | bytes 13762560 | tf_op jit(solution)/shard_map/pallas_call | solution.py:305
  157.8 2.9 %shard_map.77 = (bf16[160,5120]{1,0:T(8,128)(2,1)}, bf16[5120,256]{1,0:T(8,128)(2,1)}, bf16[5120,256]{1,0:T(8,128)(2,1)}) custom-call(bf16[160,5120]{1,0:T(8,128)(2,1)S(1)} %get-tuple-element.9.refs_0_, bf16[5120,256]{1,0:T(8,128)(2,1)S(1)} %get-tuple-element.10.refs_1_, bf16[5120,256]{1,0:T(8,128)(2,1)S(1)} %get-tuple-element.11.refs_2_), custom_call_target="tpu_custom_call" | custom-call | tf_op jit(solution)/shard_map/pallas_call | solution.py:281

commit v6 on v5

--- a/solution.py
+++ b/solution.py
@@ -294,7 +294,7 @@
     n = lax.axis_size("tensor")
     workers = lax.axis_size("dp")
     sub = 256
-    chunks = 20
+    chunks = 10
     ahead = 2
     lanes = 2
     width = features // chunks

time: 161 us -> 152 us (0.944)
  Pallas kernels: 160 us -> 152 us
    pallas_call x1, Pallas kernels: 157 us -> 149 us  [per_device(): pl.pallas_call(functools.partial(line_kernel, n, workers, chunks, lanes,...]
where the time goes in v6:
time: 152 us
  Pallas kernels  152 us (100%)
    pallas_call x1, Pallas kernels, per_device(): pl.pallas_call(functools.partial(line_kernel, n, workers, chunks, lanes,...  149 us

profile of v6, /device:TPU:0, one launch (start us, length us, event | category | flops | bytes accessed | tf_op | source)
XLA Modules:
  0.0 152.3 jit_solution(12485322811855965410)
XLA Ops:
  0.6 148.8 %shard_map.76 = (bf16[160,5120]{1,0:T(8,128)(2,1)S(1)}, bf16[5120,256]{1,0:T(8,128)(2,1)S(1)}, bf16[5120,256]{1,0:T(8,128)(2,1)S(1)}) custom-call(bf16[160,5120]{1,0:T(8,128)(2,1)} %tok_in.1, bf16[640,256]{1,0:T(8,128)(2,1)} %cot_in.1, s32[1,160]{1,0:T(1,128)} %bitcast.7, bf16[5120,256]{1,0:T(8,128)(2,1)} %w_in.1, bf16[5120,256]{1,0:T(8,128)(2,1)} %bitcast.4), custom_call_target="tpu_custom_call" | custom-call | flops 3355443200 | bytes 13762560 | tf_op jit(solution)/shard_map/pallas_call | solution.py:305
  149.4 2.9 %shard_map.77 = (bf16[160,5120]{1,0:T(8,128)(2,1)}, bf16[5120,256]{1,0:T(8,128)(2,1)}, bf16[5120,256]{1,0:T(8,128)(2,1)}) custom-call(bf16[160,5120]{1,0:T(8,128)(2,1)S(1)} %get-tuple-element.9.refs_0_, bf16[5120,256]{1,0:T(8,128)(2,1)S(1)} %get-tuple-element.10.refs_1_, bf16[5120,256]{1,0:T(8,128)(2,1)S(1)} %get-tuple-element.11.refs_2_), custom_call_target="tpu_custom_call" | custom-call | tf_op jit(solution)/shard_map/pallas_call | solution.py:281

commit v7 on v4

--- a/solution.py
+++ b/solution.py
@@ -27,14 +27,21 @@
 ):
     z = lax.axis_index("tensor")
     worker = lax.axis_index("dp")
+    first = pl.ds(0, tok_ref.shape[1] * lanes // chunks)
+    rest = pl.ds(first.size, tok_ref.shape[1] - first.size)
     loads = [
         pltpu.make_async_copy(src, dst, in_sem.at[i])
         for i, (src, dst) in enumerate(
-            ((tok_in, tok_ref), (cot_in, cot_ref), (w_in, w_ref), (mom_in, mom_ref))
+            (
+                (tok_in.at[:, first], tok_ref.at[:, first]),
+                (cot_in, cot_ref),
+                (w_in, w_ref),
+                (tok_in.at[:, rest], tok_ref.at[:, rest]),
+                (mom_in, mom_ref),
+            )
         )
     ]
-    for load in loads:
-        load.start()
+    loads[0].start()
     rows = tok_ref.shape[0]
     width = tok_ref.shape[1] // chunks
     words = sub // 32
@@ -205,6 +212,8 @@
     spread = jnp.broadcast_to(mask_in[...].astype(jnp.float32), square)
     mask_ref[...] = jnp.sum(jnp.where(diagonal, spread, 0.0), axis=1, keepdims=True)
     loads[0].wait()
+    for load in loads[1:]:
+        load.start()
     each(mask_own, 0)
 
     @pl.when(jnp.logical_and(z > 0, z < n - 1))
@@ -234,15 +243,14 @@
                     each(momentum_step, group - 1)
                 if k == min(1, n - 2):
                     each(finish_grad, group - 1)
-                if k == n - 2:
                     each(weight_step, group - 1)
 
         return carry
 
     lax.fori_loop(0, groups, one_group, 0)
     each(momentum_step, groups - 1)
+    each(finish_grad, groups - 1)
     each(weight_step, groups - 1)
-    each(finish_grad, groups - 1)
 
     def drain(j, carry):
         for way in range(2):
@@ -323,7 +331,7 @@
             dma((2, chunks, n)),
             dma((workers, chunks)),
             dma((workers, chunks)),
-            dma((4,)),
+            dma((5,)),
         ],
         compiler_params=pltpu.CompilerParams(
             collective_id=0, has_side_effects=True, vmem_limit_bytes=56 * 2**20

time: 152 us -> 153 us (level)
  no operation moved by 1% of the time
where the time goes in v7:
time: 153 us; the launch traced here: 152 us
  Pallas kernels  152 us (99%)
    pallas_call x1, Pallas kernels, per_device(): pl.pallas_call(functools.partial(line_kernel, n, workers, chunks, lanes,...  149 us

profile of v7, /device:TPU:0, one launch (start us, length us, event | category | flops | bytes accessed | tf_op | source)
XLA Modules:
  0.0 152.4 jit_solution(2179848066373435583)
XLA Ops:
  0.6 148.8 %shard_map.76 = (bf16[160,5120]{1,0:T(8,128)(2,1)S(1)}, bf16[5120,256]{1,0:T(8,128)(2,1)S(1)}, bf16[5120,256]{1,0:T(8,128)(2,1)S(1)}) custom-call(bf16[160,5120]{1,0:T(8,128)(2,1)} %tok_in.1, bf16[640,256]{1,0:T(8,128)(2,1)} %cot_in.1, s32[1,160]{1,0:T(1,128)} %bitcast.7, bf16[5120,256]{1,0:T(8,128)(2,1)} %w_in.1, bf16[5120,256]{1,0:T(8,128)(2,1)} %bitcast.4), custom_call_target="tpu_custom_call" | custom-call | flops 3355443200 | bytes 13762560 | tf_op jit(solution)/shard_map/pallas_call | solution.py:310
  149.4 2.9 %shard_map.77 = (bf16[160,5120]{1,0:T(8,128)(2,1)}, bf16[5120,256]{1,0:T(8,128)(2,1)}, bf16[5120,256]{1,0:T(8,128)(2,1)}) custom-call(bf16[160,5120]{1,0:T(8,128)(2,1)S(1)} %get-tuple-element.9.refs_0_, bf16[5120,256]{1,0:T(8,128)(2,1)S(1)} %get-tuple-element.10.refs_1_, bf16[5120,256]{1,0:T(8,128)(2,1)S(1)} %get-tuple-element.11.refs_2_), custom_call_target="tpu_custom_call" | custom-call | tf_op jit(solution)/shard_map/pallas_call | solution.py:287

commit v8 on v4

--- a/solution.py
+++ b/solution.py
@@ -190,14 +190,13 @@
 
         grad_out[:, columns(j)] = (total[...] * mask_ref[...]).astype(jnp.bfloat16)
 
-    def each(function, group):
-        def one(half, carry):
-            function(group * lanes + half)
+    def each(function, start, end):
+        def one(j, carry):
+            function(j)
             return carry
 
-        lax.fori_loop(0, lanes, one, 0)
-
-    groups = chunks // lanes
+        lax.fori_loop(start, end, one, 0)
+
     square = (rows, rows)
     diagonal = lax.broadcasted_iota(jnp.int32, square, 0) == lax.broadcasted_iota(
         jnp.int32, square, 1
@@ -205,7 +204,7 @@
     spread = jnp.broadcast_to(mask_in[...].astype(jnp.float32), square)
     mask_ref[...] = jnp.sum(jnp.where(diagonal, spread, 0.0), axis=1, keepdims=True)
     loads[0].wait()
-    each(mask_own, 0)
+    each(mask_own, 0, lanes)
 
     @pl.when(jnp.logical_and(z > 0, z < n - 1))
     def _():
@@ -215,34 +214,29 @@
     def _():
         pl.semaphore_wait(barrier, workers)
 
-    each(send_own, 0)
+    each(send_own, 0, lanes)
+
+    def next_own(j):
+        mask_own(j)
+        send_own(j)
+
+    def odd_last_slot(j):
+        slot(j, n - 2)
+        pl.when(lax.rem(j, 2) == 1)(lambda: momentum_step(j))
+
+    def finish(j):
+        pl.when(lax.rem(j, 2) == 0)(lambda: momentum_step(j))
+        finish_grad(j)
+        pl.when(j > 0)(lambda: weight_step(j - 1))
+
+    each(next_own, lanes, chunks)
     for load in loads[1:]:
         load.wait()
-
-    def one_group(group, carry):
-        for k in range(n - 1):
-            each(lambda j: slot(j, k), group)
-            if k == 0:
-                @pl.when(group + 1 < groups)
-                def _():
-                    each(mask_own, group + 1)
-                    each(send_own, group + 1)
-
-            @pl.when(group > 0)
-            def _():
-                if k == 0:
-                    each(momentum_step, group - 1)
-                if k == min(1, n - 2):
-                    each(finish_grad, group - 1)
-                if k == n - 2:
-                    each(weight_step, group - 1)
-
-        return carry
-
-    lax.fori_loop(0, groups, one_group, 0)
-    each(momentum_step, groups - 1)
-    each(weight_step, groups - 1)
-    each(finish_grad, groups - 1)
+    for k in range(n - 2):
+        each(lambda j: slot(j, k), 0, chunks)
+    each(odd_last_slot, 0, chunks)
+    each(finish, 0, chunks)
+    weight_step(chunks - 1)
 
     def drain(j, carry):
         for way in range(2):

time: 152 us -> 153 us (level)
  no operation moved by 1% of the time
where the time goes in v8:
time: 153 us
  Pallas kernels  152 us (99%)
    pallas_call x1, Pallas kernels, per_device(): pl.pallas_call(functools.partial(line_kernel, n, workers, chunks, lanes,...  149 us

profile of v8, /device:TPU:0, one launch (start us, length us, event | category | flops | bytes accessed | tf_op | source)
XLA Modules:
  0.0 152.7 jit_solution(17576985023335573904)
XLA Ops:
  0.6 149.1 %shard_map.76 = (bf16[160,5120]{1,0:T(8,128)(2,1)S(1)}, bf16[5120,256]{1,0:T(8,128)(2,1)S(1)}, bf16[5120,256]{1,0:T(8,128)(2,1)S(1)}) custom-call(bf16[160,5120]{1,0:T(8,128)(2,1)} %tok_in.1, bf16[640,256]{1,0:T(8,128)(2,1)} %cot_in.1, s32[1,160]{1,0:T(1,128)} %bitcast.7, bf16[5120,256]{1,0:T(8,128)(2,1)} %w_in.1, bf16[5120,256]{1,0:T(8,128)(2,1)} %bitcast.4), custom_call_target="tpu_custom_call" | custom-call | flops 3355443200 | bytes 13762560 | tf_op jit(solution)/shard_map/pallas_call | solution.py:296
  149.8 2.9 %shard_map.77 = (bf16[160,5120]{1,0:T(8,128)(2,1)}, bf16[5120,256]{1,0:T(8,128)(2,1)}, bf16[5120,256]{1,0:T(8,128)(2,1)}) custom-call(bf16[160,5120]{1,0:T(8,128)(2,1)S(1)} %get-tuple-element.9.refs_0_, bf16[5120,256]{1,0:T(8,128)(2,1)S(1)} %get-tuple-element.10.refs_1_, bf16[5120,256]{1,0:T(8,128)(2,1)S(1)} %get-tuple-element.11.refs_2_), custom_call_target="tpu_custom_call" | custom-call | tf_op jit(solution)/shard_map/pallas_call | solution.py:273
